TPU v7x, 256 devices: a whole 4x4x8 slice. The times are simulated.
256 devices in a mesh: vocab: 16 (over z_lo, x, core), store: 16 (over z_hi, y).
Axes of the slice: x: 4, y: 4, z: 8 (z_hi: 4, z_lo: 2; z = z_hi * 2 + z_lo), core: 2. Of those that a mesh axis runs over, the one named last changes fastest.
Arguments:
- hidden_states: bfloat16 [512, 4096], P(('vocab', 'store')), may hold values from -100 to 100, as said below
- head: bfloat16 [128256, 4096], P(('vocab', 'store')), may hold values from -0.75 to 0.75
- proj_out: float32 [128256, 64], P(('vocab', 'store')), may hold values from -6 to 6
- proj_in: bfloat16 [4096, 64], replicated, may hold values from -0.09375 to 0.09375
- store: bfloat16 [2048, 4096], P('store'), may hold values from -0.25 to 0.25
- targets: int32 [512], replicated, may hold values from 0 to 128255
Outputs:
- scores: float32 [512, 2048], P('vocab', 'store')
Inputs may be any that keep to these rules, and one draw needn't show every extreme that they name: `hidden_states`: real values; most entries of order one, some query rows a dozen times larger.
All inputs are finite; a program needn't handle non-finite values.
Results may differ from a plain program's by a relative error of at most 0.0015.
The roundings to bfloat16 on the way count: a program that leaves them out, or rounds other values in their place, can miss the bound.
Values may be sent and summed in bfloat16 or wider, within the bound.
A program may use at most 320 MiB of HBM per device.

v0:
```python
import jax
import jax.numpy as jnp
from jax import lax
from jax.sharding import PartitionSpec as P


def local(hidden_states, head, proj_out, proj_in, store, targets):
    vocab_rows = head.shape[0]
    begin = (
        lax.axis_index("vocab") * lax.axis_size("store") + lax.axis_index("store")
    ) * vocab_rows
    logits = lax.dot_general(
        lax.all_gather(hidden_states, ("vocab", "store"), axis=0, tiled=True),
        head,
        (((1,), (1,)), ((), ())),
        preferred_element_type=jnp.float32,
    )
    queries = logits.shape[0]
    share = queries // lax.axis_size("vocab")
    row_ids = begin + lax.broadcasted_iota(jnp.int32, (1, vocab_rows), 1)
    is_target = targets[:, None] == row_ids
    highest = lax.Precision.HIGHEST
    peak = lax.pmax(jnp.max(logits, axis=1), ("vocab", "store"))
    expd = jnp.exp(logits - peak[:, None])
    total = lax.psum(jnp.sum(expd, axis=1), ("vocab", "store"))
    probs = expd / total[:, None]
    weights = jnp.where(is_target, probs - 1.0, probs)
    partial_sums = jnp.dot(weights, proj_out, precision=highest, preferred_element_type=jnp.float32)
    whole = lax.psum(partial_sums, ("vocab", "store"))
    vocab_side = lax.dynamic_slice_in_dim(whole, lax.axis_index("vocab") * share, share, 0)
    own_width = jnp.dot(hidden_states, proj_in, preferred_element_type=jnp.float32)
    width_side = lax.all_gather(own_width, "store", axis=0, tiled=True)
    kron = (vocab_side[:, :, None] * width_side[:, None, :]).reshape(share, -1).astype(jnp.bfloat16)
    return lax.dot_general(
        kron, store, (((1,), (1,)), ((), ())), preferred_element_type=jnp.float32
    )


def solution(mesh):
    placed = (
        P(("vocab", "store"), None),
        P(("vocab", "store"), None),
        P(("vocab", "store"), None),
        P(),
        P("store", None),
        P(),
    )
    return jax.shard_map(
        local, mesh=mesh, in_specs=placed, out_specs=P("vocab", "store"), check_vma=False
    )
```

profile of v0, /device:TPU:32, one launch (start us, length us, event | category | flops | bytes accessed | tf_op | source)
XLA Modules:
  0.0 1141.2 jit_solution(2127063950190851730)
XLA Ops:
  6.5 0.0 copy-start
  6.5 0.0 all-gather.4.cloned.1.call-start
  6.5 0.7 all-gather.4.cloned.1.call-update
  7.3 0.0 all-reduce.2.cloned.1.call-start
  7.3 713.3 %all-gather.4.cloned.1.call-done = bf16[256,2,4096]{2,1,0:T(2,128)(2,1)} async-done(((bf16[1,2,4096]{2,1,0:T(2,128)(2,1)}), bf16[256,2,4096]{2,1,0:T(2,128)(2,1)}) %all-gather.4.cloned.1.call-update) | async-done | bytes 4194320 | tf_op jit(solution)/shard_map/all_gather | solution.py:13
  720.6 7.2 reshape.16
  727.8 0.0 copy-start.3
  727.8 0.0 copy-start.4
  727.8 5.8 fusion.10
  733.6 0.0 copy-start.1
  733.6 0.0 copy-start.2
  733.6 74.9 %pmax.7 = f32[512]{0:T(512)S(1)} all-reduce(f32[512]{0:T(512)S(1)} %get-tuple-element.5), channel_id=1, replica_groups=mesh['vocab'=16,'store'=16] {'vocab','store'}, use_global_device_ids=true, to_apply=%region_1.0 | all-reduce | flops 512 | bytes 4096 | tf_op jit(solution)/shard_map/pmax | solution.py:23
  808.6 0.2 fusion.3
  808.8 75.3 %psum.14 = f32[512]{0:T(512)S(1)} all-reduce(f32[512]{0:T(512)S(1)} %fusion.3), channel_id=1, replica_groups=mesh['vocab'=16,'store'=16] {'vocab','store'}, use_global_device_ids=true, to_apply=%region_3.0 | all-reduce | flops 512 | bytes 4096 | tf_op jit(solution)/shard_map/psum | solution.py:25
  884.1 0.0 copy-done.3
  884.1 0.0 copy-done.4
  884.1 2.6 fusion
  886.7 0.0 all-reduce.2.cloned.1.call-update
  886.8 0.0 copy-done.1
  886.8 0.0 copy-done.2
  886.8 0.2 convolution_bitcast_fusion
  887.0 41.3 %all-gather.1 = f32[16,2,64]{2,1,0:T(2,128)S(1)} all-gather(f32[1,2,64]{2,1,0:T(2,128)S(1)} %convolution_bitcast_fusion), channel_id=1, replica_groups=mesh['vocab'=16,'store'=16] {'store'}, dimensions={0}, use_global_device_ids=true | all-gather | bytes 8704 | tf_op jit(solution)/shard_map/all_gather | solution.py:32
  928.3 203.5 %all-reduce.2.cloned.1.call-done = f32[512,64]{1,0:T(8,128)} async-done(((f32[512,64]{1,0:T(8,128)}), f32[512,64]{1,0:T(8,128)}) %all-reduce.2.cloned.1.call-update) | async-done | bytes 131088 | tf_op jit(solution)/shard_map/psum | solution.py:29
  1131.8 0.7 constant_dynamic-slice_fusion
  1132.5 0.3 multiply_convert_fusion
  1132.9 0.5 convert_element_type.7
  1133.3 0.0 copy-done
  1133.3 1.1 fusion.11
  (1 shorter events, 0.0 us)
Async XLA Ops:
  6.5 1126.8 %copy-start = (bf16[128,4096]{1,0:T(8,128)(2,1)S(1)}, bf16[128,4096]{1,0:T(8,128)(2,1)}, u32[]{:S(2)}) copy-start(bf16[128,4096]{1,0:T(8,128)(2,1)} %param.10) | copy-start | bytes 3145732
  6.5 714.1 %all-gather.4.cloned.1.call-start = ((), (), s32[]{:S(2)}) async-start(), calls=%async_computation.1 | async-start | bytes 4210688 | tf_op jit(solution)/shard_map/all_gather | solution.py:13
  7.3 1124.5 %all-reduce.2.cloned.1.call-start = ((), (), s32[]{:S(2)}) async-start(), calls=%async_computation | async-start | bytes 524288 | tf_op jit(solution)/shard_map/psum | solution.py:29
  727.8 156.3 %copy-start.3 = (f32[501,64]{0,1:T(8,128)S(1)}, f32[501,64]{0,1:T(8,128)}, u32[]{:S(2)}) copy-start(f32[501,64]{0,1:T(8,128)} %param.8) | copy-start | bytes 384772
  727.8 156.3 %copy-start.4 = (s32[512]{0:T(512)S(1)}, s32[512]{0:T(512)}, u32[]{:S(2)}) copy-start(s32[512]{0:T(512)} %param.11) | copy-start | bytes 6148
  733.6 153.1 %copy-start.1 = (bf16[2,4096]{1,0:T(2,128)(2,1)S(1)}, bf16[2,4096]{1,0:T(2,128)(2,1)}, u32[]{:S(2)}) copy-start(bf16[2,4096]{1,0:T(2,128)(2,1)} %param.6) | copy-start | bytes 49156
  733.6 153.1 %copy-start.2 = (bf16[4096,64]{0,1:T(8,128)(2,1)S(1)}, bf16[4096,64]{0,1:T(8,128)(2,1)}, u32[]{:S(2)}) copy-start(bf16[4096,64]{0,1:T(8,128)(2,1)} %param.9) | copy-start | bytes 1572868
Sparse Core Ops, SparseCore 0:
  9.2 711.3 all-gather.3
  886.9 244.8 all-reduce.1
where the time goes:
time: 1140 us
  waiting for transfers between devices  917 us (80%)
  blocking collectives  192 us (17%)
  between operations  13.5 us (1%)
    all_gather x1, waiting for transfers between devices, local(): lax.all_gather(hidden_states, ('vocab', 'store'), axis=0, tiled=True)  713 us
    psum x1, waiting for transfers between devices, local(): whole = lax.psum(partial_sums, ('vocab', 'store'))  203 us
    psum x1, blocking collectives, local(): total = lax.psum(jnp.sum(expd, axis=1), ('vocab', 'store'))  75.3 us
    pmax x1, blocking collectives, local(): peak = lax.pmax(jnp.max(logits, axis=1), ('vocab', 'store'))  74.9 us
    all_gather x1, blocking collectives, local(): width_side = lax.all_gather(own_width, 'store', axis=0, tiled=True)  41.3 us
  transfers between devices with their start and end apart: 2, of which 2 were waited for; matrix products, arithmetic and copies ran while one was open for 0% of the time, Pallas kernels for 0%

commit v1 on v0

v1 whole, which is shorter than its diff:
```python
import functools

import jax
import jax.numpy as jnp
from jax import lax
from jax.experimental import pallas as pl
from jax.experimental.pallas import tpu as pltpu
from jax.sharding import PartitionSpec as P

MESH = pl.DeviceIdType.MESH
F32 = jnp.float32
BF16 = jnp.bfloat16
NT = (((1,), (1,)), ((), ()))


def kernel(
    hid, head, po, pin, store, tgt, out,
    zbuf, hbuf, head_v, po_v, w_v, pin_v, store_v, acc,
    tp, tb1, tb2, tb3, ts2, ts3, pm, rb1, rb2, rb3, rs2, rs3, wd, kron,
    lsem, csem_s, csem_r, zs, zr, gs, gr, ts, tr, rs, rr,
):
    nv, width = head.shape
    v = lax.axis_index("vocab")
    s = lax.axis_index("store")
    c = lax.rem(v, 2)
    x = lax.rem(lax.div(v, 2), 4)
    zl = lax.div(v, 8)
    zh = lax.div(s, 4)
    y = lax.rem(s, 4)
    z = zh * 2 + zl

    def dev(x_, y_, zl_, zh_, c_=None):
        c_ = c if c_ is None else c_
        return ((zl_ * 4 + x_) * 2 + c_, zh_ * 4 + y_)

    def plus(a, d, n):
        return lax.rem(a + (d + n), n)

    peer = dev(x, y, zl, zh, 1 - c)
    zpeers = []
    for d in range(1, 8):
        zz = plus(z, d, 8)
        zpeers.append(dev(x, y, lax.rem(zz, 2), lax.div(zz, 2)))
    xpeer = {d: dev(plus(x, d, 4), y, zl, zh) for d in (-1, 1)}
    ypeer = {d: dev(x, plus(y, d, 4), zl, zh) for d in (-1, 1)}
    offs = [(dx, dz) for dz in (0, 1) for dx in range(4)][1:]
    r1 = [(plus(x, dx, 4), lax.rem(zl + dz, 2)) for dx, dz in offs]
    r1dev = [dev(a, y, b, zh) for a, b in r1]
    r2dev = [dev(x, plus(y, d, 4), zl, zh) for d in (1, 2, 3)]
    r3dev = [dev(x, y, zl, plus(zh, d, 4)) for d in (1, 2, 3)]

    l_hid = pltpu.make_async_copy(hid, zbuf.at[zl * 4 + zh], lsem.at[0])
    l_po = pltpu.make_async_copy(po, po_v.at[0], lsem.at[1])
    l_head = pltpu.make_async_copy(head, head_v.at[0], lsem.at[2])
    l_pin = pltpu.make_async_copy(pin, pin_v, lsem.at[3])
    l_store = pltpu.make_async_copy(store, store_v, lsem.at[4])
    for l in (l_hid, l_po, l_head, l_pin, l_store):
        l.start()

    barrier = pltpu.get_barrier_semaphore()
    greet = zpeers + [dev(plus(x, d, 4), y, zl, zh) for d in (1, 2, 3)] + r2dev
    greet += [r1dev[k] for k, (dx, dz) in enumerate(offs) if dz and dx] + [peer]
    for other in greet:
        pl.semaphore_signal(barrier, inc=1, device_id=other, device_id_type=MESH)
    pl.semaphore_wait(barrier, len(greet))

    started = []

    def send(src, dst, ssem, rsem, to):
        copy = pltpu.make_async_remote_copy(
            src_ref=src, dst_ref=dst, send_sem=ssem, recv_sem=rsem,
            device_id=to, device_id_type=MESH,
        )
        copy.start()
        started.append(copy)
        return copy

    zcopies = [
        send(hid, zbuf.at[zl * 4 + zh], zs.at[k], zr.at[k], to)
        for k, to in enumerate(zpeers)
    ]
    c_po = send(po, po_v.at[1], csem_s.at[0], csem_r.at[0], peer)
    c_head = send(head, head_v.at[1], csem_s.at[1], csem_r.at[1], peer)

    def split(h):
        p = po_v[h]
        hi = p.astype(BF16).astype(F32)
        rest = p - hi
        mid = rest.astype(BF16).astype(F32)
        low = rest - mid
        w_v[h] = jnp.concatenate([hi, mid, low, jnp.zeros_like(p)], axis=1).astype(BF16)

    lane = lax.broadcasted_iota(jnp.int32, (1, 128), 1)
    first = lane < 64

    nq = 256
    row = lax.broadcasted_iota(jnp.int32, (nq, 1), 0)
    ry, rx, rzl, rzh, ri = (
        row // 64, (row // 16) % 4, (row // 8) % 2, (row // 2) % 4, row % 2,
    )
    query = 2 * (((rzl * 4 + rx) * 2 + c) * 16 + rzh * 4 + ry) + ri
    ids = lax.broadcasted_iota(jnp.int32, (1, 512), 1)
    wanted = jnp.sum(
        jnp.where(ids == query, tgt[...].astype(F32), 0.0), axis=1, keepdims=True
    )

    def sum_terms(a, b):
        half = a + pltpu.roll(a, 64, axis=1)
        return half + (b + pltpu.roll(b, 64, axis=1))

    def target_rows(h):
        base = (((v - c) + lax.rem(c + h, 2)) * 16 + s) * nv
        cols = (lax.broadcasted_iota(jnp.int32, (1, nv), 1) + base).astype(F32)
        hot = jnp.where(cols == wanted, 1.0, 0.0).astype(BF16)
        return jnp.dot(hot, w_v[h], preferred_element_type=F32)

    l_po.wait()
    split(0)
    t0 = target_rows(0)
    c_po.wait_recv()
    split(1)
    t01 = t0 + target_rows(1)
    t = sum_terms(t01[:, :128], t01[:, 128:]).reshape(4, 64, 128)
    tp[...] = jnp.where(first, t[:2], t[2:]).reshape(2, 4, 2, 8, 128)
    tcopies = [
        send(tp.at[:, a, b], tb1.at[k], ts.at[k], tr.at[k], r1dev[k])
        for k, (a, b) in enumerate(r1)
    ]

    l_hid.wait()
    for k in zcopies:
        k.wait_recv()
    place = y * 4 + x
    rows8 = lax.broadcasted_iota(jnp.int32, (8, 1), 0)
    for n in range(4):
        span = pl.ds(n * (width // 4), width // 4)
        halves = []
        for tile in range(2):
            made = jnp.zeros((8, width // 4), F32)
            for p in range(4):
                pair = zbuf[tile * 4 + p, :, span].astype(F32)
                for i in range(2):
                    made = jnp.where(rows8 == 2 * p + i, pair[i : i + 1], made)
            halves.append(made)
        hbuf[place, :, span] = jnp.concatenate(halves, axis=0).astype(BF16)

    half = width // 2
    quarter = width // 4

    class Order:
        def __init__(self, base, sem, apeer, bpeer, block):
            self.cols = pl.ds(base, half)
            self.part = {1: pl.ds(base, quarter), -1: pl.ds(base + quarter, quarter)}
            self.sem, self.apeer, self.bpeer, self.block = sem, apeer, bpeer, block
            self.near, self.far, self.bnear, self.bfar = {}, {}, {}, {}

        def put(self, j, block, cols, to):
            view = hbuf.at[block, :, cols]
            return send(view, view, gs.at[self.sem + j], gr.at[self.sem + j], to)

        def own(self):
            for k, d in enumerate((1, -1)):
                self.near[d] = self.put(k, self.block(0, 0), self.cols, self.apeer[d])

        def onward(self, j, da):
            for k, d in enumerate((1, -1)):
                self.bnear[da, d] = self.put(4 + j * 2 + k, self.block(da, 0), self.cols, self.bpeer[d])

        def pass_on(self, k, d):
            self.near[d].wait_recv()
            self.far[d] = self.put(2 + k, self.block(-d, 0), self.part[d], self.apeer[d])

        def bpass_on(self, j, da):
            for k, d in enumerate((1, -1)):
                self.bnear[da, d].wait_recv()
                self.bfar[da, d] = self.put(12 + j * 2 + k, self.block(da, -d), self.part[d], self.bpeer[d])

    orders = [
        Order(0, 0, xpeer, ypeer, lambda a, b: plus(y, b, 4) * 4 + plus(x, a, 4)),
        Order(half, 20, ypeer, xpeer, lambda a, b: plus(y, a, 4) * 4 + plus(x, b, 4)),
    ]
    for o in orders:
        o.own()
    for o in orders:
        o.onward(0, 0)
    for k, d in enumerate((1, -1)):
        for o in orders:
            o.pass_on(k, d)
            o.onward(1 + k, -d)

    total = tp[:, x, zl]
    for k, copy in enumerate(tcopies):
        copy.wait_recv()
        total = total + tb1[k]
    ts2[...] = total
    tcopies2 = [
        send(ts2, tb2.at[k], ts.at[7 + k], tr.at[7 + k], to) for k, to in enumerate(r2dev)
    ]

    for o in orders:
        o.bpass_on(0, 0)
    for o in orders:
        for d in (1, -1):
            o.far[d].wait_recv()
        o.onward(3, 2)
    for k, d in enumerate((1, -1)):
        for o in orders:
            o.bpass_on(1 + k, -d)

    for k, copy in enumerate(tcopies2):
        copy.wait_recv()
        total = total + tb2[k]
    ts3[...] = total
    tcopies3 = [
        send(ts3, tb3.at[k], ts.at[10 + k], tr.at[10 + k], to) for k, to in enumerate(r3dev)
    ]

    for o in orders:
        o.bpass_on(3, 2)
    for k, copy in enumerate(tcopies3):
        copy.wait_recv()
        total = total + tb3[k]
    trows = total

    l_head.wait()
    c_head.wait_recv()
    for o in orders:
        for copy in o.bfar.values():
            copy.wait_recv()

    step = 512
    acc[...] = jnp.zeros_like(acc)

    def logits(i, carry):
        span = pl.ds(pl.multiple_of(i * step, step), step)
        left = hbuf[:, :, span].reshape(nq, step)
        for h in range(2):
            acc[h] += lax.dot_general(left, head_v[h, :, span], NT, preferred_element_type=F32)
        return carry

    lax.fori_loop(0, width // step, logits, 0)

    peak = jnp.maximum(
        jnp.max(acc[0], axis=1, keepdims=True), jnp.max(acc[1], axis=1, keepdims=True)
    )
    sides = []
    denom = jnp.zeros((nq, 1), F32)
    for h in range(2):
        e = jnp.exp(acc[h] - peak)
        denom = denom + jnp.sum(e, axis=1, keepdims=True)
        hi = e.astype(BF16)
        low = (e - hi.astype(F32)).astype(BF16)
        sides.append(
            jnp.dot(hi, w_v[h], preferred_element_type=F32)
            + jnp.dot(low, w_v[h], preferred_element_type=F32)
        )
    both = sides[0] + sides[1]
    both = sum_terms(both[:, :128], both[:, 128:])
    is_peak = (lane >= 64) & (lane < 96)
    packed = jnp.where(first, both, jnp.where(is_peak, peak, denom))
    pm[...] = packed.reshape(4, 4, 2, 8, 128)
    rcopies = [
        send(pm.at[:, a, b], rb1.at[k], rs.at[k], rr.at[k], r1dev[k])
        for k, (a, b) in enumerate(r1)
    ]

    l_pin.wait()

    def widths(i, carry):
        span = pl.ds(pl.multiple_of(i * step, step), step)
        left = jnp.concatenate([hbuf[b * 4 + x, :, span] for b in range(4)], axis=0)
        return carry + jnp.dot(left, pin_v[span, :], preferred_element_type=F32)

    w = lax.fori_loop(0, width // step, widths, jnp.zeros((64, 64), F32))
    wd[...] = jnp.concatenate([w, w], axis=1).reshape(4, 2, 8, 128)
    width2 = wd[:, zl].reshape(32, 128)

    def combine(parts):
        most = parts[0]
        for p in parts[1:]:
            most = jnp.maximum(most, p)
        m = most[:, 64:65]
        out_ = None
        for p in parts:
            term = p * jnp.exp(p[:, 64:65] - m)
            out_ = term if out_ is None else out_ + term
        return jnp.where(is_peak, most, out_)

    def waited(copies, buf):
        got = []
        for k, copy in enumerate(copies):
            copy.wait_recv()
            got.append(buf[k].reshape(32, 128))
        return got

    mine = pm[:, x, zl].reshape(32, 128)
    mine = combine([mine] + waited(rcopies, rb1))
    rs2[...] = mine.reshape(4, 8, 128)
    rcopies = [send(rs2, rb2.at[k], rs.at[7 + k], rr.at[7 + k], to) for k, to in enumerate(r2dev)]
    mine = combine([mine] + waited(rcopies, rb2))
    rs3[...] = mine.reshape(4, 8, 128)
    rcopies = [send(rs3, rb3.at[k], rs.at[10 + k], rr.at[10 + k], to) for k, to in enumerate(r3dev)]
    mine = combine([mine] + waited(rcopies, rb3))

    tflat = trows.reshape(16, 128)
    side = mine / mine[:, 96:97] - jnp.concatenate([tflat, pltpu.roll(tflat, 64, axis=1)], axis=0)
    for b in range(32):
        pair = jnp.where(first, side[:, 2 * b : 2 * b + 1], side[:, 2 * b + 1 : 2 * b + 2])
        kron[:, b * 128 : (b + 1) * 128] = (pair * width2).astype(BF16)
    l_store.wait()
    scores = lax.dot_general(kron[...], store_v[...], NT, preferred_element_type=F32)
    out[...] = scores.reshape(4, 8, 128)

    for copy in started:
        copy.wait_send()


def local(hidden_states, head, proj_out, proj_in, store, targets):
    nv, width = head.shape
    vm = pltpu.VMEM
    dma = pltpu.SemaphoreType.DMA
    got = pl.pallas_call(
        kernel,
        out_shape=jax.ShapeDtypeStruct((4, 8, 128), F32),
        in_specs=[pl.BlockSpec(memory_space=pl.ANY)] * 5 + [pl.BlockSpec(memory_space=pltpu.VMEM)],
        out_specs=pl.BlockSpec(memory_space=pltpu.VMEM),
        scratch_shapes=[
            vm((8, 2, width), BF16),
            vm((16, 16, width), BF16),
            vm((2, nv, width), BF16),
            vm((2, nv, 64), F32),
            vm((2, nv, 256), BF16),
            vm((width, 64), BF16),
            vm((128, width), BF16),
            vm((2, 256, nv), F32),
            vm((2, 4, 2, 8, 128), F32),
            vm((7, 2, 8, 128), F32),
            vm((3, 2, 8, 128), F32),
            vm((3, 2, 8, 128), F32),
            vm((2, 8, 128), F32),
            vm((2, 8, 128), F32),
            vm((4, 4, 2, 8, 128), F32),
            vm((7, 4, 8, 128), F32),
            vm((3, 4, 8, 128), F32),
            vm((3, 4, 8, 128), F32),
            vm((4, 8, 128), F32),
            vm((4, 8, 128), F32),
            vm((4, 2, 8, 128), F32),
            vm((32, width), BF16),
            dma((5,)), dma((2,)), dma((2,)), dma((7,)), dma((7,)),
            dma((40,)), dma((40,)), dma((13,)), dma((13,)), dma((13,)), dma((13,)),
        ],
        compiler_params=pltpu.CompilerParams(
            collective_id=0, has_side_effects=True, vmem_limit_bytes=40 * 2**20
        ),
        cost_estimate=pl.CostEstimate(flops=2 * 10**9, bytes_accessed=10**7, transcendentals=0),
    )(hidden_states, head, proj_out, proj_in, store, targets.reshape(1, -1))
    return got.reshape(4, 4, 2, 128).transpose(1, 0, 2, 3).reshape(32, 128)


def solution(mesh):
    placed = (
        P(("vocab", "store"), None),
        P(("vocab", "store"), None),
        P(("vocab", "store"), None),
        P(),
        P("store", None),
        P(),
    )
    return jax.shard_map(
        local, mesh=mesh, in_specs=placed, out_specs=P("vocab", "store"), check_vma=False
    )
```

time: 1140 us -> 61 us (0.05)
  waiting for transfers between devices: 917 us -> 0 us
  blocking collectives: 192 us -> 0 us
  Pallas kernels: 0 us -> 52.8 us
  between operations: 13.5 us -> 0.04 us
    all_gather x1 -> x0, waiting for transfers between devices: 713 us -> none  [local(): lax.all_gather(hidden_states, ('vocab', 'store'), axis=0, tiled=True)]
    psum x1 -> x0, waiting for transfers between devices: 203 us -> none  [local(): whole = lax.psum(partial_sums, ('vocab', 'store'))]
    psum x1 -> x0, blocking collectives: 75.3 us -> none  [local(): total = lax.psum(jnp.sum(expd, axis=1), ('vocab', 'store'))]
    pmax x1 -> x0, blocking collectives: 74.9 us -> none  [local(): peak = lax.pmax(jnp.max(logits, axis=1), ('vocab', 'store'))]
    pallas_call x0 -> x1, Pallas kernels: none -> 52.8 us  [local(): pl.pallas_call(kernel, out_shape=jax.ShapeDtypeStruct((4, 8, 128), F32),...]
    all_gather x1 -> x0, blocking collectives: 41.3 us -> none  [local(): width_side = lax.all_gather(own_width, 'store', axis=0, tiled=True)]
  transfers between devices with their start and end apart: 2 -> 0, of which waited for: 2 -> 0; matrix products, arithmetic and copies ran while one was open for 0% -> 0% of each run, Pallas kernels for 0% -> 0%
where the time goes in v1:
time: 61 us; the launch traced here: 60.8 us
  Pallas kernels  52.8 us (87%)
  local copies, waits for them, and re-layouts  7.95 us (13%)
    pallas_call x1, Pallas kernels, local(): pl.pallas_call(kernel, out_shape=jax.ShapeDtypeStruct((4, 8, 128), F32),...  52.8 us
    unnamed x10, local copies, waits for them, and re-layouts  7.33 us

profile of v1, /device:TPU:32, one launch (start us, length us, event | category | flops | bytes accessed | tf_op | source)
XLA Modules:
  0.0 60.8 jit_solution(10153678416080011945)
XLA Ops:
  0.0 1.0 %copy.7.po = f32[501,64]{1,0:T(8,128)S(1)} copy(f32[501,64]{0,1:T(8,128)} %param.8) | data formatting | bytes 256512 | tf_op args[2]
  1.0 1.5 %copy.8.pin = bf16[4096,64]{1,0:T(8,128)(2,1)S(1)} copy(bf16[4096,64]{0,1:T(8,128)(2,1)} %param.9) | data formatting | bytes 1048576 | tf_op args[3]
  2.6 0.0 copy-start
  2.6 2.2 %copy-done = bf16[501,4096]{1,0:T(8,128)(2,1)S(1)} copy-done((bf16[501,4096]{1,0:T(8,128)(2,1)S(1)}, bf16[501,4096]{1,0:T(8,128)(2,1)}, u32[]{:S(2)}) %copy-start) | copy-done | bytes 4104216
  4.7 0.0 copy-start.1
  4.7 1.2 %copy-done.1 = bf16[128,4096]{1,0:T(8,128)(2,1)S(1)} copy-done((bf16[128,4096]{1,0:T(8,128)(2,1)S(1)}, bf16[128,4096]{1,0:T(8,128)(2,1)}, u32[]{:S(2)}) %copy-start.1) | copy-done | bytes 1048600
  6.0 0.0 copy-start.2
  6.0 0.7 %copy-done.2 = bf16[2,4096]{1,0:T(2,128)(2,1)S(1)} copy-done((bf16[2,4096]{1,0:T(2,128)(2,1)S(1)}, bf16[2,4096]{1,0:T(2,128)(2,1)}, u32[]{:S(2)}) %copy-start.2) | copy-done | bytes 16408
  6.7 0.0 copy-start.3
  6.7 0.7 %copy-done.3 = s32[512]{0:T(512)S(1)} copy-done((s32[512]{0:T(512)S(1)}, s32[512]{0:T(512)}, u32[]{:S(2)}) %copy-start.3) | copy-done | bytes 2072
  7.4 52.8 %shard_map.64 = f32[4,8,128]{2,1,0:T(8,128)S(1)} custom-call(bf16[2,4096]{1,0:T(2,128)(2,1)S(1)} %copy-done.2, bf16[501,4096]{1,0:T(8,128)(2,1)S(1)} %copy-done, f32[501,64]{1,0:T(8,128)S(1)} %copy.7.po, bf16[4096,64]{1,0:T(8,128)(2,1)S(1)} %copy.8.pin, bf16[128,4096]{1,0:T(8,128)(2,1)S(1)} %copy-done.1, s32[1,512]{1,0:T(1,128)S(1)} %bitcast.6), custom_call_target="tpu_custom_call" | custom-call | flops 2000000000 | bytes 10000000 | tf_op jit(solution)/shard_map/pallas_call | solution.py:322
  60.1 0.6 %copy.9 = f32[4,4,2,128]{3,2,1,0:T(2,128)} copy(f32[4,4,2,128]{3,2,0,1:T(2,128)S(1)} %bitcast.5) | data formatting | bytes 32768 | tf_op jit(solution)/shard_map/transpose | solution.py:358
Async XLA Ops:
  2.6 2.2 %copy-start = (bf16[501,4096]{1,0:T(8,128)(2,1)S(1)}, bf16[501,4096]{1,0:T(8,128)(2,1)}, u32[]{:S(2)}) copy-start(bf16[501,4096]{1,0:T(8,128)(2,1)} %head.1) | copy-start | bytes 12312580
  4.7 1.2 %copy-start.1 = (bf16[128,4096]{1,0:T(8,128)(2,1)S(1)}, bf16[128,4096]{1,0:T(8,128)(2,1)}, u32[]{:S(2)}) copy-start(bf16[128,4096]{1,0:T(8,128)(2,1)} %store.1) | copy-start | bytes 3145732
  6.0 0.7 %copy-start.2 = (bf16[2,4096]{1,0:T(2,128)(2,1)S(1)}, bf16[2,4096]{1,0:T(2,128)(2,1)}, u32[]{:S(2)}) copy-start(bf16[2,4096]{1,0:T(2,128)(2,1)} %hid.1) | copy-start | bytes 49156
  6.7 0.7 %copy-start.3 = (s32[512]{0:T(512)S(1)}, s32[512]{0:T(512)}, u32[]{:S(2)}) copy-start(s32[512]{0:T(512)} %param.11) | copy-start | bytes 6148

commit v2 on v1

--- a/solution.py
+++ b/solution.py
@@ -8,6 +8,7 @@
 from jax.sharding import PartitionSpec as P
 
 MESH = pl.DeviceIdType.MESH
+ZSHARE = 512
 F32 = jnp.float32
 BF16 = jnp.bfloat16
 NT = (((1,), (1,)), ((), ()))
@@ -15,9 +16,9 @@
 
 def kernel(
     hid, head, po, pin, store, tgt, out,
-    zbuf, hbuf, head_v, po_v, w_v, pin_v, store_v, acc,
+    tgt_v, zbuf, hbuf, head_v, po_v, w_v, pin_v, store_v, acc,
     tp, tb1, tb2, tb3, ts2, ts3, pm, rb1, rb2, rb3, rs2, rs3, wd, kron,
-    lsem, csem_s, csem_r, zs, zr, gs, gr, ts, tr, rs, rr,
+    lsem, csem_s, csem_r, zs, zr, gs, gr, ts, tr, rs, rr, dbuf, ds, dr,
 ):
     nv, width = head.shape
     v = lax.axis_index("vocab")
@@ -41,8 +42,8 @@
     for d in range(1, 8):
         zz = plus(z, d, 8)
         zpeers.append(dev(x, y, lax.rem(zz, 2), lax.div(zz, 2)))
-    xpeer = {d: dev(plus(x, d, 4), y, zl, zh) for d in (-1, 1)}
-    ypeer = {d: dev(x, plus(y, d, 4), zl, zh) for d in (-1, 1)}
+    xpeer = {d: dev(plus(x, d, 4), y, zl, zh) for d in (-1, 1, 2)}
+    ypeer = {d: dev(x, plus(y, d, 4), zl, zh) for d in (-1, 1, 2)}
     offs = [(dx, dz) for dz in (0, 1) for dx in range(4)][1:]
     r1 = [(plus(x, dx, 4), lax.rem(zl + dz, 2)) for dx, dz in offs]
     r1dev = [dev(a, y, b, zh) for a, b in r1]
@@ -50,11 +51,15 @@
     r3dev = [dev(x, y, zl, plus(zh, d, 4)) for d in (1, 2, 3)]
 
     l_hid = pltpu.make_async_copy(hid, zbuf.at[zl * 4 + zh], lsem.at[0])
+    l_last = pltpu.make_async_copy(
+        hid.at[:, pl.ds(width - ZSHARE, ZSHARE)], dbuf.at[y, x, zl * 4 + zh], lsem.at[6]
+    )
     l_po = pltpu.make_async_copy(po, po_v.at[0], lsem.at[1])
     l_head = pltpu.make_async_copy(head, head_v.at[0], lsem.at[2])
     l_pin = pltpu.make_async_copy(pin, pin_v, lsem.at[3])
     l_store = pltpu.make_async_copy(store, store_v, lsem.at[4])
-    for l in (l_hid, l_po, l_head, l_pin, l_store):
+    l_tgt = pltpu.make_async_copy(tgt, tgt_v, lsem.at[5])
+    for l in (l_hid, l_last, l_po, l_tgt, l_head, l_pin, l_store):
         l.start()
 
     barrier = pltpu.get_barrier_semaphore()
@@ -63,6 +68,10 @@
     for other in greet:
         pl.semaphore_signal(barrier, inc=1, device_id=other, device_id_type=MESH)
     pl.semaphore_wait(barrier, len(greet))
+
+    zcols = ZSHARE
+    half = (width - zcols) // 2
+    xycols, dcols = pl.ds(0, 2 * half), pl.ds(2 * half, zcols)
 
     started = []
 
@@ -75,9 +84,16 @@
         started.append(copy)
         return copy
 
+    here = zl * 4 + zh
     zcopies = [
-        send(hid, zbuf.at[zl * 4 + zh], zs.at[k], zr.at[k], to)
+        send(hid.at[:, xycols], zbuf.at[here, :, xycols], zs.at[k], zr.at[k], to)
         for k, to in enumerate(zpeers)
+    ]
+    xall = [xpeer[d] for d in (1, -1, 2)]
+    yall = [ypeer[d] for d in (1, -1, 2)]
+    dxs = [
+        send(hid.at[:, dcols], dbuf.at[y, x, here], ds.at[k], dr.at[k], to)
+        for k, to in enumerate(xall)
     ]
     c_po = send(po, po_v.at[1], csem_s.at[0], csem_r.at[0], peer)
     c_head = send(head, head_v.at[1], csem_s.at[1], csem_r.at[1], peer)
@@ -88,7 +104,7 @@
         rest = p - hi
         mid = rest.astype(BF16).astype(F32)
         low = rest - mid
-        w_v[h] = jnp.concatenate([hi, mid, low, jnp.zeros_like(p)], axis=1).astype(BF16)
+        w_v[h] = jnp.concatenate([hi, mid, low, jnp.zeros_like(p)], axis=0).astype(BF16)
 
     lane = lax.broadcasted_iota(jnp.int32, (1, 128), 1)
     first = lane < 64
@@ -100,8 +116,9 @@
     )
     query = 2 * (((rzl * 4 + rx) * 2 + c) * 16 + rzh * 4 + ry) + ri
     ids = lax.broadcasted_iota(jnp.int32, (1, 512), 1)
+    l_tgt.wait()
     wanted = jnp.sum(
-        jnp.where(ids == query, tgt[...].astype(F32), 0.0), axis=1, keepdims=True
+        jnp.where(ids == query, tgt_v[...].astype(F32), 0.0), axis=1, keepdims=True
     )
 
     def sum_terms(a, b):
@@ -112,7 +129,7 @@
         base = (((v - c) + lax.rem(c + h, 2)) * 16 + s) * nv
         cols = (lax.broadcasted_iota(jnp.int32, (1, nv), 1) + base).astype(F32)
         hot = jnp.where(cols == wanted, 1.0, 0.0).astype(BF16)
-        return jnp.dot(hot, w_v[h], preferred_element_type=F32)
+        return lax.dot_general(hot, w_v[h], NT, preferred_element_type=F32)
 
     l_po.wait()
     split(0)
@@ -127,65 +144,80 @@
         for k, (a, b) in enumerate(r1)
     ]
 
+    l_last.wait()
+    for copy in dxs:
+        copy.wait_recv()
+    dcolumn = dbuf.at[y, :, here]
+    dys = [send(dcolumn, dcolumn, ds.at[3 + k], dr.at[3 + k], to) for k, to in enumerate(yall)]
     l_hid.wait()
     for k in zcopies:
         k.wait_recv()
-    place = y * 4 + x
     rows8 = lax.broadcasted_iota(jnp.int32, (8, 1), 0)
-    for n in range(4):
-        span = pl.ds(n * (width // 4), width // 4)
+
+    def sixteen(piece):
         halves = []
         for tile in range(2):
-            made = jnp.zeros((8, width // 4), F32)
+            made = None
             for p in range(4):
-                pair = zbuf[tile * 4 + p, :, span].astype(F32)
+                pair = piece(tile * 4 + p).astype(F32)
                 for i in range(2):
-                    made = jnp.where(rows8 == 2 * p + i, pair[i : i + 1], made)
+                    row_ = jnp.broadcast_to(pair[i : i + 1], (8, pair.shape[1]))
+                    made = row_ if made is None else jnp.where(rows8 == 2 * p + i, row_, made)
             halves.append(made)
-        hbuf[place, :, span] = jnp.concatenate(halves, axis=0).astype(BF16)
-
-    half = width // 2
-    quarter = width // 4
+        return jnp.concatenate(halves, axis=0).astype(BF16)
+
+    for n in range(0, 2 * half, 512):
+        span = pl.ds(n, min(512, 2 * half - n))
+        hbuf[y, x, :, span] = sixteen(lambda p: zbuf[p, :, span])
+
+    quarter = (half // 256) * 128
 
     class Order:
         def __init__(self, base, sem, apeer, bpeer, block):
             self.cols = pl.ds(base, half)
-            self.part = {1: pl.ds(base, quarter), -1: pl.ds(base + quarter, quarter)}
+            self.part = {1: pl.ds(base, quarter), -1: pl.ds(base + quarter, half - quarter)}
             self.sem, self.apeer, self.bpeer, self.block = sem, apeer, bpeer, block
-            self.near, self.far, self.bnear, self.bfar = {}, {}, {}, {}
+            self.near, self.bnear, self.bfar = {}, {}, {}
 
         def put(self, j, block, cols, to):
-            view = hbuf.at[block, :, cols]
+            view = hbuf.at[block[0], block[1], :, cols]
             return send(view, view, gs.at[self.sem + j], gr.at[self.sem + j], to)
 
         def own(self):
-            for k, d in enumerate((1, -1)):
+            for k, d in enumerate((1, -1, 2)):
                 self.near[d] = self.put(k, self.block(0, 0), self.cols, self.apeer[d])
 
         def onward(self, j, da):
             for k, d in enumerate((1, -1)):
                 self.bnear[da, d] = self.put(4 + j * 2 + k, self.block(da, 0), self.cols, self.bpeer[d])
-
-        def pass_on(self, k, d):
-            self.near[d].wait_recv()
-            self.far[d] = self.put(2 + k, self.block(-d, 0), self.part[d], self.apeer[d])
+            if j in (3,):
+                self.bfar[da, 2] = self.put(12 + j * 2, self.block(da, 0), self.cols, self.bpeer[2])
 
         def bpass_on(self, j, da):
             for k, d in enumerate((1, -1)):
                 self.bnear[da, d].wait_recv()
+                if j in (3,):
+                    continue
                 self.bfar[da, d] = self.put(12 + j * 2 + k, self.block(da, -d), self.part[d], self.bpeer[d])
 
     orders = [
-        Order(0, 0, xpeer, ypeer, lambda a, b: plus(y, b, 4) * 4 + plus(x, a, 4)),
-        Order(half, 20, ypeer, xpeer, lambda a, b: plus(y, a, 4) * 4 + plus(x, b, 4)),
+        Order(0, 0, xpeer, ypeer, lambda a, b: (plus(y, b, 4), plus(x, a, 4))),
+        Order(half, 20, ypeer, xpeer, lambda a, b: (plus(y, a, 4), plus(x, b, 4))),
     ]
     for o in orders:
         o.own()
     for o in orders:
         o.onward(0, 0)
+    acc[...] = jnp.zeros_like(acc)
+    for copy in dys:
+        copy.wait_recv()
+    dplane = dbuf.at[:, :, here]
+    dzs = [
+        send(dplane, dplane, ds.at[6 + k], dr.at[6 + k], to) for k, to in enumerate(zpeers)
+    ]
     for k, d in enumerate((1, -1)):
         for o in orders:
-            o.pass_on(k, d)
+            o.near[d].wait_recv()
             o.onward(1 + k, -d)
 
     total = tp[:, x, zl]
@@ -200,13 +232,15 @@
     for o in orders:
         o.bpass_on(0, 0)
     for o in orders:
-        for d in (1, -1):
-            o.far[d].wait_recv()
+        o.near[2].wait_recv()
         o.onward(3, 2)
     for k, d in enumerate((1, -1)):
         for o in orders:
             o.bpass_on(1 + k, -d)
 
+    l_head.wait()
+    c_head.wait_recv()
+
     for k, copy in enumerate(tcopies2):
         copy.wait_recv()
         total = total + tb2[k]
@@ -222,37 +256,40 @@
         total = total + tb3[k]
     trows = total
 
-    l_head.wait()
-    c_head.wait_recv()
+    for copy in dzs:
+        copy.wait_recv()
+
+    def last_columns(k, carry):
+        b, a = lax.div(k, 4), lax.rem(k, 4)
+        hbuf[b, a, :, dcols] = sixteen(lambda p: dbuf[b, a, p])
+        return carry
+
+    lax.fori_loop(0, 16, last_columns, 0)
     for o in orders:
         for copy in o.bfar.values():
             copy.wait_recv()
+    for k in range(0, width, 4096):
+        span = pl.ds(k, 4096)
+        left = hbuf[:, :, :, span].reshape(nq, 4096)
+        for h in range(2):
+            part = lax.dot_general(left, head_v[h, :, span], NT, preferred_element_type=F32)
+            acc[h] = part.reshape(4, 4, 16, nv) + (acc[h] if k else 0.0)
 
     step = 512
-    acc[...] = jnp.zeros_like(acc)
-
-    def logits(i, carry):
-        span = pl.ds(pl.multiple_of(i * step, step), step)
-        left = hbuf[:, :, span].reshape(nq, step)
-        for h in range(2):
-            acc[h] += lax.dot_general(left, head_v[h, :, span], NT, preferred_element_type=F32)
-        return carry
-
-    lax.fori_loop(0, width // step, logits, 0)
-
+    flat = [acc[h].reshape(nq, nv) for h in range(2)]
     peak = jnp.maximum(
-        jnp.max(acc[0], axis=1, keepdims=True), jnp.max(acc[1], axis=1, keepdims=True)
+        jnp.max(flat[0], axis=1, keepdims=True), jnp.max(flat[1], axis=1, keepdims=True)
     )
     sides = []
     denom = jnp.zeros((nq, 1), F32)
     for h in range(2):
-        e = jnp.exp(acc[h] - peak)
+        e = jnp.exp(flat[h] - peak)
         denom = denom + jnp.sum(e, axis=1, keepdims=True)
         hi = e.astype(BF16)
         low = (e - hi.astype(F32)).astype(BF16)
         sides.append(
-            jnp.dot(hi, w_v[h], preferred_element_type=F32)
-            + jnp.dot(low, w_v[h], preferred_element_type=F32)
+            lax.dot_general(hi, w_v[h], NT, preferred_element_type=F32)
+            + lax.dot_general(low, w_v[h], NT, preferred_element_type=F32)
         )
     both = sides[0] + sides[1]
     both = sum_terms(both[:, :128], both[:, 128:])
@@ -268,8 +305,8 @@
 
     def widths(i, carry):
         span = pl.ds(pl.multiple_of(i * step, step), step)
-        left = jnp.concatenate([hbuf[b * 4 + x, :, span] for b in range(4)], axis=0)
-        return carry + jnp.dot(left, pin_v[span, :], preferred_element_type=F32)
+        left = hbuf[:, x, :, span].reshape(64, step)
+        return carry + lax.dot_general(left, pin_v[:, span], NT, preferred_element_type=F32)
 
     w = lax.fori_loop(0, width // step, widths, jnp.zeros((64, 64), F32))
     wd[...] = jnp.concatenate([w, w], axis=1).reshape(4, 2, 8, 128)
@@ -322,17 +359,18 @@
     got = pl.pallas_call(
         kernel,
         out_shape=jax.ShapeDtypeStruct((4, 8, 128), F32),
-        in_specs=[pl.BlockSpec(memory_space=pl.ANY)] * 5 + [pl.BlockSpec(memory_space=pltpu.VMEM)],
+        in_specs=[pl.BlockSpec(memory_space=pltpu.HBM)] * 6,
         out_specs=pl.BlockSpec(memory_space=pltpu.VMEM),
         scratch_shapes=[
+            vm((1, 512), jnp.int32),
             vm((8, 2, width), BF16),
-            vm((16, 16, width), BF16),
+            vm((4, 4, 16, width), BF16),
             vm((2, nv, width), BF16),
-            vm((2, nv, 64), F32),
-            vm((2, nv, 256), BF16),
-            vm((width, 64), BF16),
+            vm((2, 64, nv), F32),
+            vm((2, 256, nv), BF16),
+            vm((64, width), BF16),
             vm((128, width), BF16),
-            vm((2, 256, nv), F32),
+            vm((2, 4, 4, 16, nv), F32),
             vm((2, 4, 2, 8, 128), F32),
             vm((7, 2, 8, 128), F32),
             vm((3, 2, 8, 128), F32),
@@ -347,14 +385,15 @@
             vm((4, 8, 128), F32),
             vm((4, 2, 8, 128), F32),
             vm((32, width), BF16),
-            dma((5,)), dma((2,)), dma((2,)), dma((7,)), dma((7,)),
+            dma((7,)), dma((2,)), dma((2,)), dma((7,)), dma((7,)),
             dma((40,)), dma((40,)), dma((13,)), dma((13,)), dma((13,)), dma((13,)),
+            vm((4, 4, 8, 2, ZSHARE), BF16), dma((13,)), dma((13,)),
         ],
         compiler_params=pltpu.CompilerParams(
-            collective_id=0, has_side_effects=True, vmem_limit_bytes=40 * 2**20
+            collective_id=0, has_side_effects=True, vmem_limit_bytes=64 * 2**20 - 2**16
         ),
         cost_estimate=pl.CostEstimate(flops=2 * 10**9, bytes_accessed=10**7, transcendentals=0),
-    )(hidden_states, head, proj_out, proj_in, store, targets.reshape(1, -1))
+    )(hidden_states, head, proj_out.T, proj_in.T, store, targets.reshape(1, -1))
     return got.reshape(4, 4, 2, 128).transpose(1, 0, 2, 3).reshape(32, 128)
 
 

time: 61 us -> 50.3 us (0.82)
  local copies, waits for them, and re-layouts: 7.95 us -> 1.33 us
  Pallas kernels: 52.8 us -> 48.7 us
    unnamed x10 -> x0, local copies, waits for them, and re-layouts: 7.33 us -> none
    pallas_call x1, Pallas kernels: 52.8 us -> 48.7 us  [local(): pl.pallas_call(kernel, out_shape=jax.ShapeDtypeStruct((4, 8, 128), F32),...]
    transpose x1, local copies, waits for them, and re-layouts: 0.61 us -> 1.33 us  [local(): return got.reshape(4, 4, 2, 128).transpose(1, 0, 2, 3).reshape(32, 128)]
where the time goes in v2:
time: 50.3 us; the launch traced here: 50.1 us
  Pallas kernels  48.7 us (97%)
  local copies, waits for them, and re-layouts  1.33 us (3%)
    pallas_call x1, Pallas kernels, local(): pl.pallas_call(kernel, out_shape=jax.ShapeDtypeStruct((4, 8, 128), F32),...  48.7 us
    transpose x1, local copies, waits for them, and re-layouts, local(): return got.reshape(4, 4, 2, 128).transpose(1, 0, 2, 3).reshape(32, 128)  1.33 us

profile of v2, /device:TPU:32, one launch (start us, length us, event | category | flops | bytes accessed | tf_op | source)
XLA Modules:
  0.0 50.1 jit_solution(8355100286955482363)
XLA Ops:
  0.0 48.7 %shard_map.64 = f32[4,8,128]{2,1,0:T(8,128)} custom-call(bf16[2,4096]{1,0:T(2,128)(2,1)} %hid.1, bf16[501,4096]{1,0:T(8,128)(2,1)} %head.1, f32[64,501]{1,0:T(8,128)} %bitcast.9, bf16[64,4096]{1,0:T(8,128)(2,1)} %bitcast.8, bf16[128,4096]{1,0:T(8,128)(2,1)} %store.1, s32[1,512]{1,0:T(1,128)} %bitcast.10), custom_call_target="tpu_custom_call" | custom-call | flops 2000000000 | bytes 10000000 | tf_op jit(solution)/shard_map/pallas_call | solution.py:359
  48.7 1.3 %copy.7 = f32[4,4,2,128]{3,2,1,0:T(2,128)} copy(f32[4,4,2,128]{3,2,0,1:T(2,128)} %bitcast.7) | data formatting | bytes 32768 | tf_op jit(solution)/shard_map/transpose | solution.py:397

commit v3 on v2

--- a/solution.py
+++ b/solution.py
@@ -8,7 +8,7 @@
 from jax.sharding import PartitionSpec as P
 
 MESH = pl.DeviceIdType.MESH
-ZSHARE = 512
+ZSHARE = 768
 F32 = jnp.float32
 BF16 = jnp.bfloat16
 NT = (((1,), (1,)), ((), ()))
@@ -17,8 +17,8 @@
 def kernel(
     hid, head, po, pin, store, tgt, out,
     tgt_v, zbuf, hbuf, head_v, po_v, w_v, pin_v, store_v, acc,
-    tp, tb1, tb2, tb3, ts2, ts3, pm, rb1, rb2, rb3, rs2, rs3, wd, kron,
-    lsem, csem_s, csem_r, zs, zr, gs, gr, ts, tr, rs, rr, dbuf, ds, dr,
+    pm, rb1, rb2, rb3, rs2, rs3, wd, kron,
+    lsem, csem_s, csem_r, zs, zr, gs, gr, rs, rr, dbuf, ds, dr,
 ):
     nv, width = head.shape
     v = lax.axis_index("vocab")
@@ -39,16 +39,16 @@
 
     peer = dev(x, y, zl, zh, 1 - c)
     zpeers = []
-    for d in range(1, 8):
+    for d in (4, 3, 5, 2, 6, 1, 7):
         zz = plus(z, d, 8)
         zpeers.append(dev(x, y, lax.rem(zz, 2), lax.div(zz, 2)))
     xpeer = {d: dev(plus(x, d, 4), y, zl, zh) for d in (-1, 1, 2)}
     ypeer = {d: dev(x, plus(y, d, 4), zl, zh) for d in (-1, 1, 2)}
-    offs = [(dx, dz) for dz in (0, 1) for dx in range(4)][1:]
+    offs = [(2, 1), (1, 1), (3, 1), (2, 0), (1, 0), (3, 0), (0, 1)]
     r1 = [(plus(x, dx, 4), lax.rem(zl + dz, 2)) for dx, dz in offs]
     r1dev = [dev(a, y, b, zh) for a, b in r1]
-    r2dev = [dev(x, plus(y, d, 4), zl, zh) for d in (1, 2, 3)]
-    r3dev = [dev(x, y, zl, plus(zh, d, 4)) for d in (1, 2, 3)]
+    r2dev = [dev(x, plus(y, d, 4), zl, zh) for d in (2, 1, 3)]
+    r3dev = [dev(x, y, zl, plus(zh, d, 4)) for d in (2, 1, 3)]
 
     l_hid = pltpu.make_async_copy(hid, zbuf.at[zl * 4 + zh], lsem.at[0])
     l_last = pltpu.make_async_copy(
@@ -85,14 +85,16 @@
         return copy
 
     here = zl * 4 + zh
+    l_hid.wait()
+    l_last.wait()
     zcopies = [
-        send(hid.at[:, xycols], zbuf.at[here, :, xycols], zs.at[k], zr.at[k], to)
+        send(zbuf.at[here, :, xycols], zbuf.at[here, :, xycols], zs.at[k], zr.at[k], to)
         for k, to in enumerate(zpeers)
     ]
-    xall = [xpeer[d] for d in (1, -1, 2)]
-    yall = [ypeer[d] for d in (1, -1, 2)]
+    xall = [xpeer[d] for d in (2, 1, -1)]
+    yall = [ypeer[d] for d in (2, 1, -1)]
     dxs = [
-        send(hid.at[:, dcols], dbuf.at[y, x, here], ds.at[k], dr.at[k], to)
+        send(dbuf.at[y, x, here], dbuf.at[y, x, here], ds.at[k], dr.at[k], to)
         for k, to in enumerate(xall)
     ]
     c_po = send(po, po_v.at[1], csem_s.at[0], csem_r.at[0], peer)
@@ -138,18 +140,11 @@
     split(1)
     t01 = t0 + target_rows(1)
     t = sum_terms(t01[:, :128], t01[:, 128:]).reshape(4, 64, 128)
-    tp[...] = jnp.where(first, t[:2], t[2:]).reshape(2, 4, 2, 8, 128)
-    tcopies = [
-        send(tp.at[:, a, b], tb1.at[k], ts.at[k], tr.at[k], r1dev[k])
-        for k, (a, b) in enumerate(r1)
-    ]
-
-    l_last.wait()
+    pm[4:] = jnp.where(first, t[:2], t[2:]).reshape(2, 4, 2, 8, 128)
     for copy in dxs:
         copy.wait_recv()
     dcolumn = dbuf.at[y, :, here]
     dys = [send(dcolumn, dcolumn, ds.at[3 + k], dr.at[3 + k], to) for k, to in enumerate(yall)]
-    l_hid.wait()
     for k in zcopies:
         k.wait_recv()
     rows8 = lax.broadcasted_iota(jnp.int32, (8, 1), 0)
@@ -190,13 +185,13 @@
         def onward(self, j, da):
             for k, d in enumerate((1, -1)):
                 self.bnear[da, d] = self.put(4 + j * 2 + k, self.block(da, 0), self.cols, self.bpeer[d])
-            if j in (3,):
+            if j in (2, 3,):
                 self.bfar[da, 2] = self.put(12 + j * 2, self.block(da, 0), self.cols, self.bpeer[2])
 
         def bpass_on(self, j, da):
             for k, d in enumerate((1, -1)):
                 self.bnear[da, d].wait_recv()
-                if j in (3,):
+                if j in (2, 3,):
                     continue
                 self.bfar[da, d] = self.put(12 + j * 2 + k, self.block(da, -d), self.part[d], self.bpeer[d])
 
@@ -208,7 +203,6 @@
         o.own()
     for o in orders:
         o.onward(0, 0)
-    acc[...] = jnp.zeros_like(acc)
     for copy in dys:
         copy.wait_recv()
     dplane = dbuf.at[:, :, here]
@@ -220,15 +214,6 @@
             o.near[d].wait_recv()
             o.onward(1 + k, -d)
 
-    total = tp[:, x, zl]
-    for k, copy in enumerate(tcopies):
-        copy.wait_recv()
-        total = total + tb1[k]
-    ts2[...] = total
-    tcopies2 = [
-        send(ts2, tb2.at[k], ts.at[7 + k], tr.at[7 + k], to) for k, to in enumerate(r2dev)
-    ]
-
     for o in orders:
         o.bpass_on(0, 0)
     for o in orders:
@@ -241,21 +226,8 @@
     l_head.wait()
     c_head.wait_recv()
 
-    for k, copy in enumerate(tcopies2):
-        copy.wait_recv()
-        total = total + tb2[k]
-    ts3[...] = total
-    tcopies3 = [
-        send(ts3, tb3.at[k], ts.at[10 + k], tr.at[10 + k], to) for k, to in enumerate(r3dev)
-    ]
-
     for o in orders:
         o.bpass_on(3, 2)
-    for k, copy in enumerate(tcopies3):
-        copy.wait_recv()
-        total = total + tb3[k]
-    trows = total
-
     for copy in dzs:
         copy.wait_recv()
 
@@ -295,7 +267,7 @@
     both = sum_terms(both[:, :128], both[:, 128:])
     is_peak = (lane >= 64) & (lane < 96)
     packed = jnp.where(first, both, jnp.where(is_peak, peak, denom))
-    pm[...] = packed.reshape(4, 4, 2, 8, 128)
+    pm[:4] = packed.reshape(4, 4, 2, 8, 128)
     rcopies = [
         send(pm.at[:, a, b], rb1.at[k], rs.at[k], rr.at[k], r1dev[k])
         for k, (a, b) in enumerate(r1)
@@ -316,37 +288,46 @@
         most = parts[0]
         for p in parts[1:]:
             most = jnp.maximum(most, p)
-        m = most[:, 64:65]
-        out_ = None
+        m = most[:32, 64:65]
+        sums, rows = None, None
         for p in parts:
-            term = p * jnp.exp(p[:, 64:65] - m)
-            out_ = term if out_ is None else out_ + term
-        return jnp.where(is_peak, most, out_)
+            term = p[:32] * jnp.exp(p[:32, 64:65] - m)
+            sums = term if sums is None else sums + term
+            rows = p[32:] if rows is None else rows + p[32:]
+        return jnp.concatenate([jnp.where(is_peak, most[:32], sums), rows], axis=0)
 
     def waited(copies, buf):
         got = []
         for k, copy in enumerate(copies):
             copy.wait_recv()
-            got.append(buf[k].reshape(32, 128))
+            got.append(buf[k].reshape(48, 128))
         return got
 
-    mine = pm[:, x, zl].reshape(32, 128)
+    mine = pm[:, x, zl].reshape(48, 128)
     mine = combine([mine] + waited(rcopies, rb1))
-    rs2[...] = mine.reshape(4, 8, 128)
+    rs2[...] = mine.reshape(6, 8, 128)
     rcopies = [send(rs2, rb2.at[k], rs.at[7 + k], rr.at[7 + k], to) for k, to in enumerate(r2dev)]
     mine = combine([mine] + waited(rcopies, rb2))
-    rs3[...] = mine.reshape(4, 8, 128)
+    rs3[...] = mine.reshape(6, 8, 128)
     rcopies = [send(rs3, rb3.at[k], rs.at[10 + k], rr.at[10 + k], to) for k, to in enumerate(r3dev)]
     mine = combine([mine] + waited(rcopies, rb3))
 
-    tflat = trows.reshape(16, 128)
+    tflat, mine = mine[32:], mine[:32]
     side = mine / mine[:, 96:97] - jnp.concatenate([tflat, pltpu.roll(tflat, 64, axis=1)], axis=0)
     for b in range(32):
         pair = jnp.where(first, side[:, 2 * b : 2 * b + 1], side[:, 2 * b + 1 : 2 * b + 2])
         kron[:, b * 128 : (b + 1) * 128] = (pair * width2).astype(BF16)
     l_store.wait()
     scores = lax.dot_general(kron[...], store_v[...], NT, preferred_element_type=F32)
-    out[...] = scores.reshape(4, 8, 128)
+    pairs = lax.broadcasted_iota(jnp.int32, (8, 1), 0) // 2
+    for a in range(4):
+        made = None
+        for b in range(4):
+            turned = scores[b * 8 : b * 8 + 8]
+            if a != b:
+                turned = pltpu.roll(turned, (2 * b - 2 * a) % 8, axis=0)
+            made = turned if made is None else jnp.where(pairs == b, turned, made)
+        out[a * 8 : a * 8 + 8] = made
 
     for copy in started:
         copy.wait_send()
@@ -356,9 +337,9 @@
     nv, width = head.shape
     vm = pltpu.VMEM
     dma = pltpu.SemaphoreType.DMA
-    got = pl.pallas_call(
+    return pl.pallas_call(
         kernel,
-        out_shape=jax.ShapeDtypeStruct((4, 8, 128), F32),
+        out_shape=jax.ShapeDtypeStruct((32, 128), F32),
         in_specs=[pl.BlockSpec(memory_space=pltpu.HBM)] * 6,
         out_specs=pl.BlockSpec(memory_space=pltpu.VMEM),
         scratch_shapes=[
@@ -371,22 +352,16 @@
             vm((64, width), BF16),
             vm((128, width), BF16),
             vm((2, 4, 4, 16, nv), F32),
-            vm((2, 4, 2, 8, 128), F32),
-            vm((7, 2, 8, 128), F32),
-            vm((3, 2, 8, 128), F32),
-            vm((3, 2, 8, 128), F32),
-            vm((2, 8, 128), F32),
-            vm((2, 8, 128), F32),
-            vm((4, 4, 2, 8, 128), F32),
-            vm((7, 4, 8, 128), F32),
-            vm((3, 4, 8, 128), F32),
-            vm((3, 4, 8, 128), F32),
-            vm((4, 8, 128), F32),
-            vm((4, 8, 128), F32),
+            vm((6, 4, 2, 8, 128), F32),
+            vm((7, 6, 8, 128), F32),
+            vm((3, 6, 8, 128), F32),
+            vm((3, 6, 8, 128), F32),
+            vm((6, 8, 128), F32),
+            vm((6, 8, 128), F32),
             vm((4, 2, 8, 128), F32),
             vm((32, width), BF16),
             dma((7,)), dma((2,)), dma((2,)), dma((7,)), dma((7,)),
-            dma((40,)), dma((40,)), dma((13,)), dma((13,)), dma((13,)), dma((13,)),
+            dma((40,)), dma((40,)), dma((13,)), dma((13,)),
             vm((4, 4, 8, 2, ZSHARE), BF16), dma((13,)), dma((13,)),
         ],
         compiler_params=pltpu.CompilerParams(
@@ -394,8 +369,6 @@
         ),
         cost_estimate=pl.CostEstimate(flops=2 * 10**9, bytes_accessed=10**7, transcendentals=0),
     )(hidden_states, head, proj_out.T, proj_in.T, store, targets.reshape(1, -1))
-    return got.reshape(4, 4, 2, 128).transpose(1, 0, 2, 3).reshape(32, 128)
-
 
 def solution(mesh):
     placed = (

time: 50.3 us -> 47 us (0.934)
  Pallas kernels: 48.7 us -> 45.5 us
    pallas_call x1, Pallas kernels: 48.7 us -> 45.5 us  [local(): pl.pallas_call(kernel, out_shape=jax.ShapeDtypeStruct((32, 128), F32), in...]
    transpose x1 -> x0, local copies, waits for them, and re-layouts: 1.33 us -> none  [local(): return got.reshape(4, 4, 2, 128).transpose(1, 0, 2, 3).reshape(32, 128)]
    unnamed x0 -> x1, local copies, waits for them, and re-layouts: none -> 1.32 us
where the time goes in v3:
time: 47 us; the launch traced here: 46.8 us
  Pallas kernels  45.5 us (97%)
  local copies, waits for them, and re-layouts  1.32 us (3%)
    pallas_call x1, Pallas kernels, local(): pl.pallas_call(kernel, out_shape=jax.ShapeDtypeStruct((32, 128), F32), in...  45.5 us
    unnamed x1, local copies, waits for them, and re-layouts  1.32 us

profile of v3, /device:TPU:32, one launch (start us, length us, event | category | flops | bytes accessed | tf_op | source)
XLA Modules:
  0.0 46.8 jit_solution(3974082111061580998)
XLA Ops:
  0.0 45.5 %shard_map.64 = f32[32,128]{1,0:T(8,128)} custom-call(bf16[2,4096]{1,0:T(2,128)(2,1)} %hid.1, bf16[501,4096]{1,0:T(8,128)(2,1)} %head.1, f32[64,501]{1,0:T(8,128)} %bitcast.4, bf16[64,4096]{1,0:T(8,128)(2,1)} %bitcast.3, bf16[128,4096]{1,0:T(8,128)(2,1)} %store.1, s32[1,512]{1,0:T(1,128)} %bitcast.5), custom_call_target="tpu_custom_call" | custom-call | flops 2000000000 | bytes 10000000 | tf_op jit(solution)/shard_map/pallas_call | solution.py:340
  45.5 1.3 %copy.8 = f32[32,128]{1,0:T(8,128)} copy(f32[32,128]{1,0:T(8,128)} %shard_map.64) | data formatting | bytes 32768

commit v4 on v3

--- a/solution.py
+++ b/solution.py
@@ -18,7 +18,7 @@
     hid, head, po, pin, store, tgt, out,
     tgt_v, zbuf, hbuf, head_v, po_v, w_v, pin_v, store_v, acc,
     pm, rb1, rb2, rb3, rs2, rs3, wd, kron,
-    lsem, csem_s, csem_r, zs, zr, gs, gr, rs, rr, dbuf, ds, dr,
+    lsem, csem_s, csem_r, zs, zr, gs, gr, ts, tr, rs, rr, dbuf, ds, dr,
 ):
     nv, width = head.shape
     v = lax.axis_index("vocab")
@@ -161,10 +161,6 @@
             halves.append(made)
         return jnp.concatenate(halves, axis=0).astype(BF16)
 
-    for n in range(0, 2 * half, 512):
-        span = pl.ds(n, min(512, 2 * half - n))
-        hbuf[y, x, :, span] = sixteen(lambda p: zbuf[p, :, span])
-
     quarter = (half // 256) * 128
 
     class Order:
@@ -199,7 +195,10 @@
         Order(0, 0, xpeer, ypeer, lambda a, b: (plus(y, b, 4), plus(x, a, 4))),
         Order(half, 20, ypeer, xpeer, lambda a, b: (plus(y, a, 4), plus(x, b, 4))),
     ]
-    for o in orders:
+    for o, base in zip(orders, (0, half)):
+        for n in range(base, base + half, half // 2 // 128 * 128):
+            span = pl.ds(n, min(half // 2 // 128 * 128, base + half - n))
+            hbuf[y, x, :, span] = sixteen(lambda p: zbuf[p, :, span])
         o.own()
     for o in orders:
         o.onward(0, 0)
@@ -215,10 +214,10 @@
             o.onward(1 + k, -d)
 
     for o in orders:
-        o.bpass_on(0, 0)
-    for o in orders:
         o.near[2].wait_recv()
         o.onward(3, 2)
+    for o in orders:
+        o.bpass_on(0, 0)
     for k, d in enumerate((1, -1)):
         for o in orders:
             o.bpass_on(1 + k, -d)
@@ -240,12 +239,14 @@
     for o in orders:
         for copy in o.bfar.values():
             copy.wait_recv()
-    for k in range(0, width, 4096):
-        span = pl.ds(k, 4096)
-        left = hbuf[:, :, :, span].reshape(nq, 4096)
-        for h in range(2):
-            part = lax.dot_general(left, head_v[h, :, span], NT, preferred_element_type=F32)
-            acc[h] = part.reshape(4, 4, 16, nv) + (acc[h] if k else 0.0)
+    tcopies = [
+        send(pm.at[pl.ds(4, 2), a, b], rb1.at[k, pl.ds(4, 2)], ts.at[k], tr.at[k], r1dev[k])
+        for k, (a, b) in enumerate(r1)
+    ]
+    left = hbuf[...].reshape(nq, width)
+    for h in range(2):
+        part = lax.dot_general(left, head_v[h], NT, preferred_element_type=F32)
+        acc[h] = part.reshape(4, 4, 16, nv)
 
     step = 512
     flat = [acc[h].reshape(nq, nv) for h in range(2)]
@@ -269,7 +270,9 @@
     packed = jnp.where(first, both, jnp.where(is_peak, peak, denom))
     pm[:4] = packed.reshape(4, 4, 2, 8, 128)
     rcopies = [
-        send(pm.at[:, a, b], rb1.at[k], rs.at[k], rr.at[k], r1dev[k])
+        send(
+            pm.at[pl.ds(0, 4), a, b], rb1.at[k, pl.ds(0, 4)], rs.at[k], rr.at[k], r1dev[k]
+        )
         for k, (a, b) in enumerate(r1)
     ]
 
@@ -303,6 +306,8 @@
             got.append(buf[k].reshape(48, 128))
         return got
 
+    for copy in tcopies:
+        copy.wait_recv()
     mine = pm[:, x, zl].reshape(48, 128)
     mine = combine([mine] + waited(rcopies, rb1))
     rs2[...] = mine.reshape(6, 8, 128)
@@ -361,7 +366,7 @@
             vm((4, 2, 8, 128), F32),
             vm((32, width), BF16),
             dma((7,)), dma((2,)), dma((2,)), dma((7,)), dma((7,)),
-            dma((40,)), dma((40,)), dma((13,)), dma((13,)),
+            dma((40,)), dma((40,)), dma((7,)), dma((7,)), dma((13,)), dma((13,)),
             vm((4, 4, 8, 2, ZSHARE), BF16), dma((13,)), dma((13,)),
         ],
         compiler_params=pltpu.CompilerParams(

time: 47 us -> 46.5 us (0.989)
  Pallas kernels: 45.5 us -> 45 us
where the time goes in v4:
time: 46.5 us; the launch traced here: 46.4 us
  Pallas kernels  45 us (97%)
  local copies, waits for them, and re-layouts  1.32 us (3%)
    pallas_call x1, Pallas kernels, local(): pl.pallas_call(kernel, out_shape=jax.ShapeDtypeStruct((32, 128), F32), in...  45 us
    unnamed x1, local copies, waits for them, and re-layouts  1.32 us

profile of v4, /device:TPU:32, one launch (start us, length us, event | category | flops | bytes accessed | tf_op | source)
XLA Modules:
  0.0 46.4 jit_solution(17576927268995964681)
XLA Ops:
  0.0 45.0 %shard_map.64 = f32[32,128]{1,0:T(8,128)} custom-call(bf16[2,4096]{1,0:T(2,128)(2,1)} %hid.1, bf16[501,4096]{1,0:T(8,128)(2,1)} %head.1, f32[64,501]{1,0:T(8,128)} %bitcast.4, bf16[64,4096]{1,0:T(8,128)(2,1)} %bitcast.3, bf16[128,4096]{1,0:T(8,128)(2,1)} %store.1, s32[1,512]{1,0:T(1,128)} %bitcast.5), custom_call_target="tpu_custom_call" | custom-call | flops 2000000000 | bytes 10000000 | tf_op jit(solution)/shard_map/pallas_call | solution.py:345
  45.0 1.3 %copy.8 = f32[32,128]{1,0:T(8,128)} copy(f32[32,128]{1,0:T(8,128)} %shard_map.64) | data formatting | bytes 32768

commit v5 on v4

--- a/solution.py
+++ b/solution.py
@@ -50,6 +50,11 @@
     r2dev = [dev(x, plus(y, d, 4), zl, zh) for d in (2, 1, 3)]
     r3dev = [dev(x, y, zl, plus(zh, d, 4)) for d in (2, 1, 3)]
 
+    barrier = pltpu.get_barrier_semaphore()
+    greet = zpeers + [dev(plus(x, d, 4), y, zl, zh) for d in (1, 2, 3)] + r2dev
+    greet += [r1dev[k] for k, (dx, dz) in enumerate(offs) if dz and dx] + [peer]
+    for other in greet:
+        pl.semaphore_signal(barrier, inc=1, device_id=other, device_id_type=MESH)
     l_hid = pltpu.make_async_copy(hid, zbuf.at[zl * 4 + zh], lsem.at[0])
     l_last = pltpu.make_async_copy(
         hid.at[:, pl.ds(width - ZSHARE, ZSHARE)], dbuf.at[y, x, zl * 4 + zh], lsem.at[6]
@@ -62,11 +67,6 @@
     for l in (l_hid, l_last, l_po, l_tgt, l_head, l_pin, l_store):
         l.start()
 
-    barrier = pltpu.get_barrier_semaphore()
-    greet = zpeers + [dev(plus(x, d, 4), y, zl, zh) for d in (1, 2, 3)] + r2dev
-    greet += [r1dev[k] for k, (dx, dz) in enumerate(offs) if dz and dx] + [peer]
-    for other in greet:
-        pl.semaphore_signal(barrier, inc=1, device_id=other, device_id_type=MESH)
     pl.semaphore_wait(barrier, len(greet))
 
     zcols = ZSHARE
@@ -140,7 +140,9 @@
     split(1)
     t01 = t0 + target_rows(1)
     t = sum_terms(t01[:, :128], t01[:, 128:]).reshape(4, 64, 128)
-    pm[4:] = jnp.where(first, t[:2], t[2:]).reshape(2, 4, 2, 8, 128)
+    t = jnp.where(first, t[:2], t[2:]).reshape(2, 4, 2, 8, 128)
+    for k in range(2):
+        pm[:, :, 4 + k] = t[k]
     for copy in dxs:
         copy.wait_recv()
     dcolumn = dbuf.at[y, :, here]
@@ -240,7 +242,7 @@
         for copy in o.bfar.values():
             copy.wait_recv()
     tcopies = [
-        send(pm.at[pl.ds(4, 2), a, b], rb1.at[k, pl.ds(4, 2)], ts.at[k], tr.at[k], r1dev[k])
+        send(pm.at[a, b, pl.ds(4, 2)], rb1.at[k, pl.ds(4, 2)], ts.at[k], tr.at[k], r1dev[k])
         for k, (a, b) in enumerate(r1)
     ]
     left = hbuf[...].reshape(nq, width)
@@ -268,10 +270,12 @@
     both = sum_terms(both[:, :128], both[:, 128:])
     is_peak = (lane >= 64) & (lane < 96)
     packed = jnp.where(first, both, jnp.where(is_peak, peak, denom))
-    pm[:4] = packed.reshape(4, 4, 2, 8, 128)
+    packed = packed.reshape(4, 4, 2, 8, 128)
+    for k in range(4):
+        pm[:, :, k] = packed[k]
     rcopies = [
         send(
-            pm.at[pl.ds(0, 4), a, b], rb1.at[k, pl.ds(0, 4)], rs.at[k], rr.at[k], r1dev[k]
+            pm.at[a, b, pl.ds(0, 4)], rb1.at[k, pl.ds(0, 4)], rs.at[k], rr.at[k], r1dev[k]
         )
         for k, (a, b) in enumerate(r1)
     ]
@@ -291,34 +295,51 @@
         most = parts[0]
         for p in parts[1:]:
             most = jnp.maximum(most, p)
-        m = most[:32, 64:65]
-        sums, rows = None, None
+        m = most[:, 64:65]
+        sums = None
         for p in parts:
-            term = p[:32] * jnp.exp(p[:32, 64:65] - m)
+            term = p * jnp.exp(p[:, 64:65] - m)
             sums = term if sums is None else sums + term
-            rows = p[32:] if rows is None else rows + p[32:]
-        return jnp.concatenate([jnp.where(is_peak, most[:32], sums), rows], axis=0)
+        return jnp.where(is_peak, most, sums)
 
     def waited(copies, buf):
         got = []
         for k, copy in enumerate(copies):
             copy.wait_recv()
-            got.append(buf[k].reshape(48, 128))
+            got.append(buf[k, :4].reshape(32, 128))
         return got
 
-    for copy in tcopies:
-        copy.wait_recv()
-    mine = pm[:, x, zl].reshape(48, 128)
+    def target_sum(total, copies, buf):
+        for k, copy in enumerate(copies):
+            copy.wait_recv()
+            total = total + buf[k, 4:].reshape(16, 128)
+        return total
+
+    sums_of, rows_of = pl.ds(0, 4), pl.ds(4, 2)
+
+    def step_on(held, bufs, first_sem, sems, part, to_all):
+        return [
+            send(held.at[part], bufs.at[k, part], sems[0].at[first_sem + k], sems[1].at[first_sem + k], to)
+            for k, to in enumerate(to_all)
+        ]
+
+    rows = target_sum(pm[x, zl, 4:].reshape(16, 128), tcopies, rb1)
+    rs2[4:] = rows.reshape(2, 8, 128)
+    tcopies = step_on(rs2, rb2, 7, (ts, tr), rows_of, r2dev)
+    mine = pm[x, zl, :4].reshape(32, 128)
     mine = combine([mine] + waited(rcopies, rb1))
-    rs2[...] = mine.reshape(6, 8, 128)
-    rcopies = [send(rs2, rb2.at[k], rs.at[7 + k], rr.at[7 + k], to) for k, to in enumerate(r2dev)]
+    rs2[:4] = mine.reshape(4, 8, 128)
+    rcopies = step_on(rs2, rb2, 7, (rs, rr), sums_of, r2dev)
+    rows = target_sum(rows, tcopies, rb2)
+    rs3[4:] = rows.reshape(2, 8, 128)
+    tcopies = step_on(rs3, rb3, 10, (ts, tr), rows_of, r3dev)
     mine = combine([mine] + waited(rcopies, rb2))
-    rs3[...] = mine.reshape(6, 8, 128)
-    rcopies = [send(rs3, rb3.at[k], rs.at[10 + k], rr.at[10 + k], to) for k, to in enumerate(r3dev)]
+    rs3[:4] = mine.reshape(4, 8, 128)
+    rcopies = step_on(rs3, rb3, 10, (rs, rr), sums_of, r3dev)
+    rows = target_sum(rows, tcopies, rb3)
     mine = combine([mine] + waited(rcopies, rb3))
 
-    tflat, mine = mine[32:], mine[:32]
-    side = mine / mine[:, 96:97] - jnp.concatenate([tflat, pltpu.roll(tflat, 64, axis=1)], axis=0)
+    side = mine / mine[:, 96:97] - jnp.concatenate([rows, pltpu.roll(rows, 64, axis=1)], axis=0)
     for b in range(32):
         pair = jnp.where(first, side[:, 2 * b : 2 * b + 1], side[:, 2 * b + 1 : 2 * b + 2])
         kron[:, b * 128 : (b + 1) * 128] = (pair * width2).astype(BF16)
@@ -357,7 +378,7 @@
             vm((64, width), BF16),
             vm((128, width), BF16),
             vm((2, 4, 4, 16, nv), F32),
-            vm((6, 4, 2, 8, 128), F32),
+            vm((4, 2, 6, 8, 128), F32),
             vm((7, 6, 8, 128), F32),
             vm((3, 6, 8, 128), F32),
             vm((3, 6, 8, 128), F32),
@@ -366,7 +387,7 @@
             vm((4, 2, 8, 128), F32),
             vm((32, width), BF16),
             dma((7,)), dma((2,)), dma((2,)), dma((7,)), dma((7,)),
-            dma((40,)), dma((40,)), dma((7,)), dma((7,)), dma((13,)), dma((13,)),
+            dma((40,)), dma((40,)), dma((13,)), dma((13,)), dma((13,)), dma((13,)),
             vm((4, 4, 8, 2, ZSHARE), BF16), dma((13,)), dma((13,)),
         ],
         compiler_params=pltpu.CompilerParams(

time: 46.5 us -> 46.4 us (level)
  no operation moved by 1% of the time
where the time goes in v5:
time: 46.4 us; the launch traced here: 46.2 us
  Pallas kernels  44.9 us (97%)
  local copies, waits for them, and re-layouts  1.32 us (3%)
    pallas_call x1, Pallas kernels, local(): pl.pallas_call(kernel, out_shape=jax.ShapeDtypeStruct((32, 128), F32), in...  44.9 us
    unnamed x1, local copies, waits for them, and re-layouts  1.32 us

profile of v5, /device:TPU:32, one launch (start us, length us, event | category | flops | bytes accessed | tf_op | source)
XLA Modules:
  0.0 46.2 jit_solution(6310151311271603556)
XLA Ops:
  0.0 44.9 %shard_map.64 = f32[32,128]{1,0:T(8,128)} custom-call(bf16[2,4096]{1,0:T(2,128)(2,1)} %hid.1, bf16[501,4096]{1,0:T(8,128)(2,1)} %head.1, f32[64,501]{1,0:T(8,128)} %bitcast.4, bf16[64,4096]{1,0:T(8,128)(2,1)} %bitcast.3, bf16[128,4096]{1,0:T(8,128)(2,1)} %store.1, s32[1,512]{1,0:T(1,128)} %bitcast.5), custom_call_target="tpu_custom_call" | custom-call | flops 2000000000 | bytes 10000000 | tf_op jit(solution)/shard_map/pallas_call | solution.py:366
  44.9 1.3 %copy.8 = f32[32,128]{1,0:T(8,128)} copy(f32[32,128]{1,0:T(8,128)} %shard_map.64) | data formatting | bytes 32768

commit v6 on v5

--- a/solution.py
+++ b/solution.py
@@ -64,7 +64,7 @@
     l_pin = pltpu.make_async_copy(pin, pin_v, lsem.at[3])
     l_store = pltpu.make_async_copy(store, store_v, lsem.at[4])
     l_tgt = pltpu.make_async_copy(tgt, tgt_v, lsem.at[5])
-    for l in (l_hid, l_last, l_po, l_tgt, l_head, l_pin, l_store):
+    for l in (l_hid, l_last, l_po, l_tgt):
         l.start()
 
     pl.semaphore_wait(barrier, len(greet))
@@ -97,6 +97,8 @@
         send(dbuf.at[y, x, here], dbuf.at[y, x, here], ds.at[k], dr.at[k], to)
         for k, to in enumerate(xall)
     ]
+    for l in (l_head, l_pin, l_store):
+        l.start()
     c_po = send(po, po_v.at[1], csem_s.at[0], csem_r.at[0], peer)
     c_head = send(head, head_v.at[1], csem_s.at[1], csem_r.at[1], peer)
 

time: 46.4 us -> 46.4 us (level)
  no operation moved by 1% of the time
where the time goes in v6:
time: 46.4 us; the launch traced here: 46.2 us
  Pallas kernels  44.9 us (97%)
  local copies, waits for them, and re-layouts  1.32 us (3%)
    pallas_call x1, Pallas kernels, local(): pl.pallas_call(kernel, out_shape=jax.ShapeDtypeStruct((32, 128), F32), in...  44.9 us
    unnamed x1, local copies, waits for them, and re-layouts  1.32 us

profile of v6, /device:TPU:32, one launch (start us, length us, event | category | flops | bytes accessed | tf_op | source)
XLA Modules:
  0.0 46.2 jit_solution(15884946319947308005)
XLA Ops:
  0.0 44.9 %shard_map.64 = f32[32,128]{1,0:T(8,128)} custom-call(bf16[2,4096]{1,0:T(2,128)(2,1)} %hid.1, bf16[501,4096]{1,0:T(8,128)(2,1)} %head.1, f32[64,501]{1,0:T(8,128)} %bitcast.4, bf16[64,4096]{1,0:T(8,128)(2,1)} %bitcast.3, bf16[128,4096]{1,0:T(8,128)(2,1)} %store.1, s32[1,512]{1,0:T(1,128)} %bitcast.5), custom_call_target="tpu_custom_call" | custom-call | flops 2000000000 | bytes 10000000 | tf_op jit(solution)/shard_map/pallas_call | solution.py:368
  44.9 1.3 %copy.8 = f32[32,128]{1,0:T(8,128)} copy(f32[32,128]{1,0:T(8,128)} %shard_map.64) | data formatting | bytes 32768
